TPU v7x, 32 devices: a whole 2x2x4 slice. The times are simulated.
32 devices in a mesh: lat: 4 (over z), lon: 8 (over y, x, core).
Axes of the slice: x: 2, y: 2, z: 4, core: 2. Of those that a mesh axis runs over, the one named last changes fastest.
Arguments:
- level_tokens: float32 [24, 96, 13, 512], P('lat', None, None, 'lon'), may hold values from -6 to 6
- latent_queries: float32 [4, 512], replicated, may hold values from -48 to 48
- agg_key: float32 [512, 512], replicated, may hold values from -0.25 to 0.25
- agg_value: float32 [512, 512], replicated, may hold values from -0.25 to 0.25
- agg_out: float32 [512, 512], replicated, may hold values from -0.25 to 0.25
- attn_gain: float32 [512], replicated, may hold values from 0.7 to 5
- window_qkv: float32 [512, 1536], replicated, may hold values from -0.25 to 0.25
- window_proj: float32 [512, 512], replicated, may hold values from -0.25 to 0.25
- mlp_gain: float32 [512], replicated, may hold values from 0.25 to 1.75
- mlp_in: float32 [512, 2048], replicated, may hold values from -0.25 to 0.25
- mlp_out: float32 [2048, 512], replicated, may hold values from -0.125 to 0.125
- level_queries: float32 [13, 512], replicated, may hold values from -48 to 48
- dec_key: float32 [512, 512], replicated, may hold values from -0.25 to 0.25
- dec_value: float32 [512, 512], replicated, may hold values from -0.25 to 0.25
- dec_out: float32 [512, 512], replicated, may hold values from -0.25 to 0.25
Outputs:
- decoded: float32 [24, 96, 13, 512], P('lat', 'lon')
All inputs are finite; a program needn't handle non-finite values.
Results may differ from a plain program's by a relative error of at most 0.0003.
Values sent between devices are 32-bit elements; how exact they have to be, the bound alone decides.
A program may use at most 256 MiB of HBM per device.

v0:
```python
import functools

import jax
import jax.numpy as jnp
from jax import lax
from jax.experimental import pallas as pl
from jax.experimental.pallas import tpu as pltpu
from jax.sharding import PartitionSpec as P

D = 512
HEADS = 16
HEAD_SIZE = 32
LEVELS = 13
LATENT = 4
SCALE = 1.0 / HEAD_SIZE**0.5
HALF = 40
QUAD = 24
F32 = jnp.float32
BF16 = jnp.bfloat16
PARAMS = pltpu.CompilerParams(vmem_limit_bytes=58 * 1024 * 1024)
VM = pl.BlockSpec(memory_space=pltpu.VMEM)


def split(x):
    hi = x.astype(BF16)
    return hi, (x - hi.astype(F32)).astype(BF16)


def mm(a, b, dims=(((1,), (0,)), ((), ()))):
    return lax.dot_general(a, b, dims, preferred_element_type=F32)


def dot3(a, b):
    ah, al = split(a)
    bh, bl = split(b)
    return mm(ah, bh) + (mm(ah, bl) + mm(al, bh))


def dot6(a, b):
    return jnp.dot(a, b, precision=lax.Precision.HIGHEST, preferred_element_type=F32)


def head_of(shape, dim):
    return lax.broadcasted_iota(jnp.int32, shape, dim) // HEAD_SIZE


def folded(key, queries, count):
    head = head_of((HEADS, D), 1) == lax.broadcasted_iota(jnp.int32, (HEADS, D), 0)
    spread = jnp.concatenate(
        [jnp.where(head, queries[q : q + 1, :] * SCALE, 0.0) for q in range(count)], axis=0
    )
    return lax.dot_general(
        key,
        spread,
        (((1,), (1,)), ((), ())),
        precision=lax.Precision.HIGHEST,
        preferred_element_type=F32,
    )


def widen(q, width):
    row = lax.broadcasted_iota(jnp.int32, (width, D), 0)
    return jnp.where(row == q * HEADS + head_of((width, D), 1), 1.0, 0.0).astype(BF16)


def layer_norm(values, gain):
    center = values - jnp.mean(values, -1, keepdims=True)
    spread = jnp.mean(center * center, -1, keepdims=True)
    return center * lax.rsqrt(spread + 1e-05) * gain


def pack_kernel(count, tokens, out):
    spare = 128 - 2 * tokens.shape[2]
    for level in range(LEVELS):
        for row in range(3):
            parts = [tokens[row, level], tokens[row + 3, level]]
            if spare:
                parts.append(jnp.zeros((spare, tokens.shape[3]), F32))
            pair = jnp.concatenate(parts, axis=0)
            turned = pair.T
            for dest in range(count):
                for half in range(2):
                    start = dest * 12 + half * 6
                    at = half * 18 + row * 6
                    out[dest, level, at : at + 6, :] = turned[start : start + 6, :]
        for dest in range(count):
            out[dest, level, 36:40, :] = jnp.zeros((4, 128), F32)


def agg_kernel(got, queries, key, value, out_w, q00, q01, q10, q11, tok, val):
    ways = got.shape[0] // 4
    channels = 128 // ways
    lane = lax.broadcasted_iota(jnp.int32, (HALF, 128), 1) // channels
    for level in range(LEVELS):
        for t in range(4):
            for g in range(2):
                joined = jnp.zeros((HALF, 128), F32)
                for i in range(ways):
                    block = got[ways * t + i, level]
                    if i != g:
                        block = pltpu.roll(block, (i - g) * channels % 128, 1)
                    joined = jnp.where(lane == i, block, joined)
                at = level * 80 + g * HALF
                tok[at : at + HALF, 128 * t : 128 * t + 128] = joined
    x = tok[...]
    scores = dot6(x, folded(key[...], queries[...], LATENT)).reshape(LEVELS, 80, LATENT * HEADS)
    val[...] = dot3(x, value[...])
    expo = jnp.exp(scores - jnp.max(scores, axis=0, keepdims=True))
    weights = (expo / jnp.sum(expo, axis=0, keepdims=True)).reshape(LEVELS * 80, LATENT * HEADS)
    wh, wl = split(weights)
    mixed = []
    for c in range(LATENT):
        spread = widen(c, LATENT * HEADS)
        wide = (mm(wh, spread) + mm(wl, spread)) * val[...]
        mixed.append(jnp.sum(wide.reshape(LEVELS, 80, D), axis=0))
    latent = dot3(jnp.concatenate(mixed, axis=0), out_w[...])
    for c in range(LATENT):
        for g, pair in enumerate(((q00, q01), (q10, q11))):
            base = c * 80 + g * 40
            block = latent[base : base + 40]
            for half, ref in enumerate(pair):
                ref[c, 0:18, :] = block[half * 18 : half * 18 + 18]
                ref[c, 18:24, :] = jnp.zeros((6, D), F32)


def window_kernel(
    last, q11, q10, q01, q00, attn_gain, qkv, proj, mlp_gain, mlp_in, mlp_out, o11, o10, o01, o00,
    joined, att,
):
    side = 4 * QUAD
    latent = jnp.concatenate(
        [ref[c] for c in range(LATENT) for ref in (q11, q10, q01, q00)], axis=0
    )
    joined[...] = dot3(layer_norm(latent, attn_gain[...]), qkv[...])
    edge = lax.axis_index("lat") == last
    for c0, depth in ((0, 1), (1, 2), (3, 1)):
        n = side * depth
        rows = slice(c0 * side, c0 * side + n)
        qi = lax.broadcasted_iota(jnp.int32, (n, n), 0) % side // (2 * QUAD)
        kc = lax.broadcasted_iota(jnp.int32, (n, n), 1)
        cut = jnp.where(edge, 1, 0) * jnp.where(qi != kc % side // (2 * QUAD), 1, 0)
        ok = (kc % QUAD < 18) & (cut == 0)
        for t in range(4):
            q = joined[rows, 128 * t : 128 * t + 128] * SCALE
            k = joined[rows, D + 128 * t : D + 128 * t + 128]
            v = joined[rows, 2 * D + 128 * t : 2 * D + 128 * t + 128]
            kh, kl = split(k)
            vh, vl = split(v)
            total = jnp.zeros((n, 128), F32)
            for h in range(4):
                mine = head_of((n, 128), 1) == h
                qh, ql = split(jnp.where(mine, q, 0.0))
                nt = (((1,), (1,)), ((), ()))
                s = mm(qh, kh, nt) + (mm(qh, kl, nt) + mm(ql, kh, nt))
                s = jnp.where(ok, s, -1e30)
                e = jnp.exp(s - jnp.max(s, -1, keepdims=True))
                eh, el = split(e)
                r = mm(eh, vh) + (mm(eh, vl) + mm(el, vh))
                total = jnp.where(mine, r / jnp.sum(e, -1, keepdims=True), total)
            att[rows, 128 * t : 128 * t + 128] = total
    mid = latent + dot3(att[...], proj[...])
    hidden = jax.nn.gelu(dot3(layer_norm(mid, mlp_gain[...]), mlp_in[...]))
    done = mid + dot3(hidden, mlp_out[...])
    for c in range(LATENT):
        for i, ref in enumerate((o11, o10, o01, o00)):
            base = c * side + i * QUAD
            ref[c] = done[base : base + QUAD]


def decode_kernel(q00, q01, q10, q11, queries, key, value, out_w, out, mixed):
    side = 4 * QUAD
    x = jnp.concatenate([ref[c] for c in range(LATENT) for ref in (q00, q01, q10, q11)], axis=0)
    width = LEVELS * HEADS
    scores = dot6(x, folded(key[...], queries[...], LEVELS)).reshape(LATENT, side, width)
    val = dot3(x, value[...])
    expo = jnp.exp(scores - jnp.max(scores, axis=0, keepdims=True))
    weights = (expo / jnp.sum(expo, axis=0, keepdims=True)).reshape(LATENT * side, width)
    wh, wl = split(weights)
    for level in range(LEVELS):
        spread = widen(level, width)
        wide = (mm(wh, spread) + mm(wl, spread)) * val
        mixed[level * side : level * side + side] = jnp.sum(wide.reshape(LATENT, side, D), axis=0)
    done = dot3(mixed[...], out_w[...])
    for level in range(LEVELS):
        for g in range(2):
            for half in range(2):
                for row in range(3):
                    at = level * side + (2 * g + half) * QUAD + row * 6
                    out[3 * g + row, 6 * half : 6 * half + 6, level, :] = done[at : at + 6]


def on_device(
    level_tokens,
    latent_queries,
    agg_key,
    agg_value,
    agg_out,
    attn_gain,
    window_qkv,
    window_proj,
    mlp_gain,
    mlp_in,
    mlp_out,
    level_queries,
    dec_key,
    dec_value,
    dec_out,
):
    n_lat, n_lon = lax.axis_size("lat"), lax.axis_size("lon")
    packed = pl.pallas_call(
        functools.partial(pack_kernel, n_lon),
        out_shape=jax.ShapeDtypeStruct((n_lon, LEVELS, HALF, 128), F32),
        in_specs=[VM],
        out_specs=VM,
        compiler_params=PARAMS,
    )(level_tokens.transpose(0, 2, 3, 1))
    got = lax.all_to_all(packed, "lon", split_axis=0, concat_axis=0, tiled=True)
    quad = jax.ShapeDtypeStruct((LATENT, QUAD, D), F32)
    q00, q01, q10, q11 = pl.pallas_call(
        agg_kernel,
        out_shape=[quad] * 4,
        in_specs=[VM] * 5,
        out_specs=[VM] * 4,
        scratch_shapes=[pltpu.VMEM((LEVELS * 80, D), F32), pltpu.VMEM((LEVELS * 80, D), F32)],
        compiler_params=PARAMS,
    )(got, latent_queries, agg_key, agg_value, agg_out)

    lon = [(j, (j - 1) % n_lon) for j in range(n_lon)]
    lat = [(i, (i - 1) % n_lat) for i in range(n_lat)]
    both = [
        (i * n_lon + j, (i - 1) % n_lat * n_lon + (j - 1) % n_lon)
        for i in range(n_lat)
        for j in range(n_lon)
    ]

    def back(pairs):
        return [(target, source) for source, target in pairs]

    q00 = lax.ppermute(q00, ("lat", "lon"), both)
    q01 = lax.ppermute(q01, "lat", lat)
    q10 = lax.ppermute(q10, "lon", lon)
    q11, q10, q01, q00 = pl.pallas_call(
        functools.partial(window_kernel, n_lat - 1),
        out_shape=[quad] * 4,
        in_specs=[VM] * 10,
        out_specs=[VM] * 4,
        scratch_shapes=[
            pltpu.VMEM((4 * QUAD * LATENT, 3 * D), F32),
            pltpu.VMEM((4 * QUAD * LATENT, D), F32),
        ],
        compiler_params=PARAMS,
    )(
        q11, q10, q01, q00, attn_gain.reshape(1, D), window_qkv, window_proj,
        mlp_gain.reshape(1, D), mlp_in, mlp_out,
    )
    q00 = lax.ppermute(q00, ("lat", "lon"), back(both))
    q01 = lax.ppermute(q01, "lat", back(lat))
    q10 = lax.ppermute(q10, "lon", back(lon))
    return pl.pallas_call(
        decode_kernel,
        out_shape=jax.ShapeDtypeStruct((6, 12, LEVELS, D), F32),
        in_specs=[VM] * 8,
        out_specs=VM,
        scratch_shapes=[pltpu.VMEM((LEVELS * 4 * QUAD, D), F32)],
        compiler_params=PARAMS,
    )(q00, q01, q10, q11, level_queries, dec_key, dec_value, dec_out)


def solution(mesh):
    in_specs = (P("lat", None, None, "lon"),) + (P(),) * 14
    out_specs = P("lat", "lon", None, None)
    return jax.shard_map(
        on_device, mesh=mesh, in_specs=in_specs, out_specs=out_specs, check_vma=False
    )
```

profile of v0, /device:TPU:0, one launch (start us, length us, event | category | flops | bytes accessed | tf_op | source)
XLA Modules:
  0.0 117.9 jit_solution(7062504679333342066)
XLA Ops:
  0.0 3.8 %shard_map.145 = f32[8,13,40,128]{3,2,1,0:T(8,128)} custom-call(f32[6,13,64,96]{3,2,1,0:T(8,128)} %bitcast.3), custom_call_target="tpu_custom_call" | custom-call | tf_op jit(solution)/shard_map/pallas_call | solution.py:210
  3.8 32.2 %all_to_all.5.got = f32[8,13,40,128]{3,2,1,0:T(8,128)} all-to-all(f32[8,13,40,128]{3,2,1,0:T(8,128)} %shard_map.145), channel_id=1, replica_groups=mesh['lat'=4,'lon'=8] {'lon'}, dimensions={0} | all-to-all | bytes 4259840 | tf_op jit(solution)/shard_map/all_to_all | solution.py:217
  36.0 13.2 %shard_map.146 = (f32[4,24,512]{2,1,0:T(8,128)}, f32[4,24,512]{2,1,0:T(8,128)}, f32[4,24,512]{2,1,0:T(8,128)}, f32[4,24,512]{2,1,0:T(8,128)}) custom-call(f32[8,13,40,128]{3,2,1,0:T(8,128)} %all_to_all.5.got, f32[4,512]{1,0:T(4,128)} %queries.2, f32[512,512]{1,0:T(8,128)} %key.2, f32[512,512]{1,0:T(8,128)} %value.2, f32[512,512]{1,0:T(8,128)} %out_w.2), custom_call_target="tpu_custom_call" | custom-call | tf_op jit(solution)/shard_map/pallas_call | solution.py:219
  49.2 0.1 collective-permute-start
  49.3 4.1 %collective-permute-start.1 = (f32[4,24,512]{2,1,0:T(8,128)}, f32[4,24,512]{2,1,0:T(8,128)S(1)}, u32[]{:S(2)}, u32[]{:S(2)}) collective-permute-start(f32[4,24,512]{2,1,0:T(8,128)} %get-tuple-element.15), channel_id=1, source_target_pairs={{0,24},{8,0},{16,8},{24,16},{1,25},{9,1},{17,9},{25,17},{2,26},{10... | collective-permute-start | bytes 589832 | tf_op jit(solution)/shard_map/ppermute | solution.py:240
  53.4 0.2 collective-permute-start.2
  53.6 0.0 collective-permute-done.q10
  53.6 0.0 copy-start.3
  53.6 5.4 %collective-permute-done.1.q01 = f32[4,24,512]{2,1,0:T(8,128)S(1)} collective-permute-done((f32[4,24,512]{2,1,0:T(8,128)}, f32[4,24,512]{2,1,0:T(8,128)S(1)}, u32[]{:S(2)}, u32[]{:S(2)}) %collective-permute-start.1) | collective-permute-done | bytes 196640 | tf_op jit(solution)/shard_map/ppermute | solution.py:240
  58.9 0.0 copy-start.4
  59.0 3.7 %collective-permute-done.2.q00 = f32[4,24,512]{2,1,0:T(8,128)S(1)} collective-permute-done((f32[4,24,512]{2,1,0:T(8,128)}, f32[4,24,512]{2,1,0:T(8,128)S(1)}, u32[]{:S(2)}, u32[]{:S(2)}) %collective-permute-start.2) | collective-permute-done | bytes 196640 | tf_op jit(solution)/shard_map/ppermute | solution.py:239
  62.7 0.0 copy-start.5
  62.7 0.0 copy-done.3
  62.7 0.0 copy-done.4
  62.7 0.7 copy-done.5
  63.4 27.7 %shard_map.147 = (f32[4,24,512]{2,1,0:T(8,128)}, f32[4,24,512]{2,1,0:T(8,128)}, f32[4,24,512]{2,1,0:T(8,128)}, f32[4,24,512]{2,1,0:T(8,128)}) custom-call(f32[4,24,512]{2,1,0:T(8,128)} %get-tuple-element.13.q11, f32[4,24,512]{2,1,0:T(8,128)} %copy-done.3, f32[4,24,512]{2,1,0:T(8,128)} %copy-done.4, f32[4,24,512]{2,1,0:T(8,128)} %copy-done.5, ...), custom_call_target="tpu_custom_call" | custom-call | tf_op jit(solution)/shard_map/pallas_call | solution.py:242
  91.0 0.0 collective-permute-start.3
  91.0 1.3 %collective-permute-start.4 = (f32[4,24,512]{2,1,0:T(8,128)}, f32[4,24,512]{2,1,0:T(8,128)S(1)}, u32[]{:S(2)}, u32[]{:S(2)}) collective-permute-start(f32[4,24,512]{2,1,0:T(8,128)} %get-tuple-element.18), channel_id=1, source_target_pairs={{24,0},{0,8},{8,16},{16,24},{25,1},{1,9},{9,17},{17,25},{26,2},{2,... | collective-permute-start | bytes 589832 | tf_op jit(solution)/shard_map/ppermute | solution.py:257
  92.4 0.0 collective-permute-start.5
  92.4 9.8 %collective-permute-done.3.q00 = f32[4,24,512]{2,1,0:T(8,128)S(1)} collective-permute-done((f32[4,24,512]{2,1,0:T(8,128)}, f32[4,24,512]{2,1,0:T(8,128)S(1)}, u32[]{:S(2)}, u32[]{:S(2)}) %collective-permute-start.3) | collective-permute-done | bytes 196640 | tf_op jit(solution)/shard_map/ppermute | solution.py:256
  102.2 0.0 copy-start
  102.2 2.3 %collective-permute-done.4.q01 = f32[4,24,512]{2,1,0:T(8,128)S(1)} collective-permute-done((f32[4,24,512]{2,1,0:T(8,128)}, f32[4,24,512]{2,1,0:T(8,128)S(1)}, u32[]{:S(2)}, u32[]{:S(2)}) %collective-permute-start.4) | collective-permute-done | bytes 196640 | tf_op jit(solution)/shard_map/ppermute | solution.py:257
  104.5 0.0 copy-start.1
  104.5 0.0 collective-permute-done.5.q10
  104.5 0.0 copy-start.2
  104.5 0.0 copy-done
  104.5 0.7 copy-done.1
  105.2 0.1 copy-done.2
  105.3 12.7 %shard_map.148 = f32[6,12,13,512]{3,2,1,0:T(8,128)} custom-call(f32[4,24,512]{2,1,0:T(8,128)} %copy-done, f32[4,24,512]{2,1,0:T(8,128)} %copy-done.1, f32[4,24,512]{2,1,0:T(8,128)} %copy-done.2, f32[4,24,512]{2,1,0:T(8,128)} %get-tuple-element.20.q11, f32[13,512]{1,0:T(8,128)} %queries.3, f32[512,512]{1,0:T(8,128)} %key.3, f32[512,512]{1,0:T(8,128)} %value.3, ...), custom_call_target="tpu_custom_call" | custom-call | tf_op jit(solution)/shard_map/pallas_call | solution.py:259
Async XLA Ops:
  49.2 4.4 %collective-permute-start = (f32[4,24,512]{2,1,0:T(8,128)}, f32[4,24,512]{2,1,0:T(8,128)S(1)}, u32[]{:S(2)}, u32[]{:S(2)}) collective-permute-start(f32[4,24,512]{2,1,0:T(8,128)} %get-tuple-element.14), channel_id=1, source_target_pairs={{0,7},{1,0},{2,1},{3,2},{4,3},{5,4},{6,5},{7,6},{8,15},{9,8},{10,9... | collective-permute-start | bytes 589832 | tf_op jit(solution)/shard_map/ppermute | solution.py:241
  49.3 9.7 %collective-permute-start.1 = (f32[4,24,512]{2,1,0:T(8,128)}, f32[4,24,512]{2,1,0:T(8,128)S(1)}, u32[]{:S(2)}, u32[]{:S(2)}) collective-permute-start(f32[4,24,512]{2,1,0:T(8,128)} %get-tuple-element.15), channel_id=1, source_target_pairs={{0,24},{8,0},{16,8},{24,16},{1,25},{9,1},{17,9},{25,17},{2,26},{10... | collective-permute-start | bytes 589832 | tf_op jit(solution)/shard_map/ppermute | solution.py:240
  53.4 9.3 %collective-permute-start.2 = (f32[4,24,512]{2,1,0:T(8,128)}, f32[4,24,512]{2,1,0:T(8,128)S(1)}, u32[]{:S(2)}, u32[]{:S(2)}) collective-permute-start(f32[4,24,512]{2,1,0:T(8,128)} %get-tuple-element.16), channel_id=1, source_target_pairs={{0,31},{1,24},{2,25},{3,26},{4,27},{5,28},{6,29},{7,30},{8,7},{9,0... | collective-permute-start | bytes 589832 | tf_op jit(solution)/shard_map/ppermute | solution.py:239
  53.6 9.1 %copy-start.3 = (f32[4,24,512]{2,1,0:T(8,128)}, f32[4,24,512]{2,1,0:T(8,128)S(1)}, u32[]{:S(2)}) copy-start(f32[4,24,512]{2,1,0:T(8,128)S(1)} %collective-permute-done.q10) | copy-start | bytes 589828
  58.9 3.7 %copy-start.4 = (f32[4,24,512]{2,1,0:T(8,128)}, f32[4,24,512]{2,1,0:T(8,128)S(1)}, u32[]{:S(2)}) copy-start(f32[4,24,512]{2,1,0:T(8,128)S(1)} %collective-permute-done.1.q01) | copy-start | bytes 589828
  62.7 0.7 copy-start.5
  91.0 11.1 %collective-permute-start.3 = (f32[4,24,512]{2,1,0:T(8,128)}, f32[4,24,512]{2,1,0:T(8,128)S(1)}, u32[]{:S(2)}, u32[]{:S(2)}) collective-permute-start(f32[4,24,512]{2,1,0:T(8,128)} %get-tuple-element.17), channel_id=1, source_target_pairs={{31,0},{24,1},{25,2},{26,3},{27,4},{28,5},{29,6},{30,7},{7,8},{0,9... | collective-permute-start | bytes 589832 | tf_op jit(solution)/shard_map/ppermute | solution.py:256
  91.0 13.5 %collective-permute-start.4 = (f32[4,24,512]{2,1,0:T(8,128)}, f32[4,24,512]{2,1,0:T(8,128)S(1)}, u32[]{:S(2)}, u32[]{:S(2)}) collective-permute-start(f32[4,24,512]{2,1,0:T(8,128)} %get-tuple-element.18), channel_id=1, source_target_pairs={{24,0},{0,8},{8,16},{16,24},{25,1},{1,9},{9,17},{17,25},{26,2},{2,... | collective-permute-start | bytes 589832 | tf_op jit(solution)/shard_map/ppermute | solution.py:257
  92.4 12.1 %collective-permute-start.5 = (f32[4,24,512]{2,1,0:T(8,128)}, f32[4,24,512]{2,1,0:T(8,128)S(1)}, u32[]{:S(2)}, u32[]{:S(2)}) collective-permute-start(f32[4,24,512]{2,1,0:T(8,128)} %get-tuple-element.19), channel_id=1, source_target_pairs={{7,0},{0,1},{1,2},{2,3},{3,4},{4,5},{5,6},{6,7},{15,8},{8,9},{9,10... | collective-permute-start | bytes 589832 | tf_op jit(solution)/shard_map/ppermute | solution.py:258
  102.2 2.3 %copy-start = (f32[4,24,512]{2,1,0:T(8,128)}, f32[4,24,512]{2,1,0:T(8,128)S(1)}, u32[]{:S(2)}) copy-start(f32[4,24,512]{2,1,0:T(8,128)S(1)} %collective-permute-done.3.q00) | copy-start | bytes 589828
  104.5 0.7 copy-start.1
  104.5 0.8 copy-start.2
where the time goes:
time: 118 us
  Pallas kernels  57.3 us (49%)
  blocking collectives  32.2 us (27%)
  waiting for transfers between devices  21.2 us (18%)
  starting transfers between devices  5.74 us (5%)
  local copies, waits for them, and re-layouts  1.45 us (1%)
    all_to_all x1, blocking collectives, on_device(): got = lax.all_to_all(packed, 'lon', split_axis=0, concat_axis=0, tiled=True)  32.2 us
    pallas_call x1, Pallas kernels, on_device(): pl.pallas_call(functools.partial(window_kernel, n_lat - 1), out_shape=[qu...  27.7 us
    pallas_call x1, Pallas kernels, on_device(): pl.pallas_call(agg_kernel, out_shape=[quad] * 4, in_specs=[VM] * 5, out_s...  13.2 us
    pallas_call x1, Pallas kernels, on_device(): pl.pallas_call(decode_kernel, out_shape=jax.ShapeDtypeStruct((6, 12, LEVE...  12.7 us
    ppermute x1, waiting for transfers between devices, on_device(): q00 = lax.ppermute(q00, ('lat', 'lon'), back(both))  9.79 us
    ppermute x1, waiting for transfers between devices, on_device(): q01 = lax.ppermute(q01, 'lat', lat)  5.36 us
    ppermute x1, starting transfers between devices, on_device(): q01 = lax.ppermute(q01, 'lat', lat)  4.12 us
    pallas_call x1, Pallas kernels, on_device(): pl.pallas_call(functools.partial(pack_kernel, n_lon), out_shape=jax.Shape...  3.78 us
  transfers between devices with their start and end apart: 6, of which 4 were waited for; matrix products, arithmetic and copies ran while one was open for 0% of the time, Pallas kernels for 0%

commit v1 on v0

--- a/solution.py
+++ b/solution.py
@@ -17,7 +17,8 @@
 QUAD = 24
 F32 = jnp.float32
 BF16 = jnp.bfloat16
-PARAMS = pltpu.CompilerParams(vmem_limit_bytes=58 * 1024 * 1024)
+LIMIT = 58 * 1024 * 1024
+PARAMS = pltpu.CompilerParams(vmem_limit_bytes=LIMIT)
 VM = pl.BlockSpec(memory_space=pltpu.VMEM)
 
 
@@ -69,29 +70,113 @@
     return center * lax.rsqrt(spread + 1e-05) * gain
 
 
-def pack_kernel(count, tokens, out):
+MESH = pl.DeviceIdType.MESH
+CHUNKS = ((0, 4), (4, 7), (7, 10), (10, 13))
+
+
+def places(step):
+    n_lat, n_lon = lax.axis_size("lat"), lax.axis_size("lon")
+    a, b = lax.axis_index("lat"), lax.axis_index("lon")
+    a1, b1 = lax.rem(a + step + n_lat, n_lat), lax.rem(b + step + n_lon, n_lon)
+    return ((a1, b1), (a1, b), (a, b1))
+
+
+def greet(devices):
+    barrier = pltpu.get_barrier_semaphore()
+    for device in devices:
+        pl.semaphore_signal(barrier, inc=1, device_id=device, device_id_type=MESH)
+    pl.semaphore_wait(barrier, len(devices))
+
+
+def hand_over(step, sent, landed, send_sem, recv_sem):
+    copies = [
+        pltpu.make_async_remote_copy(
+            src_ref=sent.at[i],
+            dst_ref=landed.at[i],
+            send_sem=send_sem.at[i],
+            recv_sem=recv_sem.at[i],
+            device_id=device,
+            device_id_type=MESH,
+        )
+        for i, device in enumerate(places(step))
+    ]
+    for copy in copies:
+        copy.start()
+    return copies
+
+
+def agg_kernel(
+    tokens, queries, key, value, out_w, q00, q01, q10, q11,
+    packed, got, tok, val, score, vhi, vlo, sent, landed,
+    pack_send, pack_recv, own_sem, quad_send, quad_recv,
+):
+    count = lax.axis_size("lon")
+    a, b = lax.axis_index("lat"), lax.axis_index("lon")
+    partners = [(a, lax.rem(b + k, count)) for k in range(1, count)]
+    greet(partners + list(places(-1)[:2]) + list(places(1)[:2]))
+
     spare = 128 - 2 * tokens.shape[2]
-    for level in range(LEVELS):
+    channels = tokens.shape[2]
+    ways = 128 // channels
+    order = [count // 2 + (k // 2 + 1) * (1 if k % 2 else -1) for k in range(count - 2)]
+    order = [count // 2] + [k for k in order if 0 < k < count]
+    order = order + [k for k in range(1, count) if k not in order]
+
+    def pack_level(level, carry):
         for row in range(3):
             parts = [tokens[row, level], tokens[row + 3, level]]
             if spare:
                 parts.append(jnp.zeros((spare, tokens.shape[3]), F32))
-            pair = jnp.concatenate(parts, axis=0)
-            turned = pair.T
+            turned = jnp.concatenate(parts, axis=0).T
             for dest in range(count):
                 for half in range(2):
                     start = dest * 12 + half * 6
                     at = half * 18 + row * 6
-                    out[dest, level, at : at + 6, :] = turned[start : start + 6, :]
+                    packed[dest, level, at : at + 6, :] = turned[start : start + 6, :]
         for dest in range(count):
-            out[dest, level, 36:40, :] = jnp.zeros((4, 128), F32)
-
-
-def agg_kernel(got, queries, key, value, out_w, q00, q01, q10, q11, tok, val):
-    ways = got.shape[0] // 4
-    channels = 128 // ways
+            packed[dest, level, 36:40, :] = jnp.zeros((4, 128), F32)
+        return carry
+
+    def remote(c, k):
+        low, high = CHUNKS[c]
+        to = lax.rem(b + k, count)
+        return pltpu.make_async_remote_copy(
+            src_ref=packed.at[to, low:high],
+            dst_ref=got.at[b, low:high],
+            send_sem=pack_send.at[c, k],
+            recv_sem=pack_recv.at[c, k],
+            device_id=(a, to),
+            device_id_type=MESH,
+        )
+
+    def arriving(c, k):
+        low, high = CHUNKS[c]
+        origin = lax.rem(b - k + count, count)
+        return pltpu.make_async_remote_copy(
+            src_ref=packed.at[origin, low:high],
+            dst_ref=got.at[origin, low:high],
+            send_sem=pack_send.at[c, k],
+            recv_sem=pack_recv.at[c, k],
+            device_id=(a, origin),
+            device_id_type=MESH,
+        )
+
+    def own(c):
+        low, high = CHUNKS[c]
+        return pltpu.make_async_copy(
+            packed.at[b, low:high], got.at[b, low:high], own_sem.at[c]
+        )
+
+    for c, (low, high) in enumerate(CHUNKS):
+        lax.fori_loop(low, high, pack_level, 0)
+        for k in order:
+            remote(c, k).start()
+        own(c).start()
+    fold = folded(key[...], queries[...], LATENT)
+    vhi[...], vlo[...] = split(value[...])
     lane = lax.broadcasted_iota(jnp.int32, (HALF, 128), 1) // channels
-    for level in range(LEVELS):
+
+    def unpack_level(level, carry):
         for t in range(4):
             for g in range(2):
                 joined = jnp.zeros((HALF, 128), F32)
@@ -100,11 +185,20 @@
                     if i != g:
                         block = pltpu.roll(block, (i - g) * channels % 128, 1)
                     joined = jnp.where(lane == i, block, joined)
-                at = level * 80 + g * HALF
-                tok[at : at + HALF, 128 * t : 128 * t + 128] = joined
-    x = tok[...]
-    scores = dot6(x, folded(key[...], queries[...], LATENT)).reshape(LEVELS, 80, LATENT * HEADS)
-    val[...] = dot3(x, value[...])
+                tok[level, g * HALF : g * HALF + HALF, 128 * t : 128 * t + 128] = joined
+        return carry
+
+    for c, (low, high) in enumerate(CHUNKS):
+        for k in order:
+            arriving(c, k).wait_recv()
+        own(c).wait()
+        lax.fori_loop(low, high, unpack_level, 0)
+        x = tok[low:high].reshape((high - low) * 80, D)
+        score[low:high] = dot6(x, fold).reshape(high - low, 80, LATENT * HEADS)
+        xh, xl = split(x)
+        v = mm(xh, vhi[...]) + (mm(xh, vlo[...]) + mm(xl, vhi[...]))
+        val[low * 80 : high * 80] = v
+    scores = score[...]
     expo = jnp.exp(scores - jnp.max(scores, axis=0, keepdims=True))
     weights = (expo / jnp.sum(expo, axis=0, keepdims=True)).reshape(LEVELS * 80, LATENT * HEADS)
     wh, wl = split(weights)
@@ -115,18 +209,30 @@
         mixed.append(jnp.sum(wide.reshape(LEVELS, 80, D), axis=0))
     latent = dot3(jnp.concatenate(mixed, axis=0), out_w[...])
     for c in range(LATENT):
-        for g, pair in enumerate(((q00, q01), (q10, q11))):
-            base = c * 80 + g * 40
-            block = latent[base : base + 40]
-            for half, ref in enumerate(pair):
-                ref[c, 0:18, :] = block[half * 18 : half * 18 + 18]
-                ref[c, 18:24, :] = jnp.zeros((6, D), F32)
+        for i, ref in enumerate((sent.at[0], sent.at[1], sent.at[2], q11)):
+            base = c * 80 + i // 2 * HALF + i % 2 * 18
+            ref[c, 0:18, :] = latent[base : base + 18]
+            ref[c, 18:24, :] = jnp.zeros((6, D), F32)
+    copies = hand_over(-1, sent, landed, quad_send, quad_recv)
+    for c in range(len(CHUNKS)):
+        for k in order:
+            remote(c, k).wait_send()
+    for copy, i, ref in zip(copies, range(3), (q00, q01, q10)):
+        copy.wait()
+        ref[...] = landed[i]
 
 
 def window_kernel(
-    last, q11, q10, q01, q00, attn_gain, qkv, proj, mlp_gain, mlp_in, mlp_out, o11, o10, o01, o00,
-    joined, att,
+    last, q11, q10, q01, q00, attn_gain, qkv, proj, mlp_gain, hbm_in, hbm_out, o11, o10, o01, o00,
+    joined, att, mlp_in, mlp_out, sent, landed, load_sem, quad_send, quad_recv,
 ):
+    loads = [
+        pltpu.make_async_copy(hbm_in, mlp_in, load_sem.at[0]),
+        pltpu.make_async_copy(hbm_out, mlp_out, load_sem.at[1]),
+    ]
+    for load in loads:
+        load.start()
+    greet(list(places(-1)) + list(places(1)))
     side = 4 * QUAD
     latent = jnp.concatenate(
         [ref[c] for c in range(LATENT) for ref in (q11, q10, q01, q00)], axis=0
@@ -159,12 +265,18 @@
                 total = jnp.where(mine, r / jnp.sum(e, -1, keepdims=True), total)
             att[rows, 128 * t : 128 * t + 128] = total
     mid = latent + dot3(att[...], proj[...])
+    for load in loads:
+        load.wait()
     hidden = jax.nn.gelu(dot3(layer_norm(mid, mlp_gain[...]), mlp_in[...]))
     done = mid + dot3(hidden, mlp_out[...])
     for c in range(LATENT):
-        for i, ref in enumerate((o11, o10, o01, o00)):
+        for i, ref in enumerate((o11, sent.at[2], sent.at[1], sent.at[0])):
             base = c * side + i * QUAD
             ref[c] = done[base : base + QUAD]
+    copies = hand_over(1, sent, landed, quad_send, quad_recv)
+    for copy, i, ref in zip(copies, range(3), (o00, o01, o10)):
+        copy.wait()
+        ref[...] = landed[i]
 
 
 def decode_kernel(q00, q01, q10, q11, queries, key, value, out_w, out, mixed):
@@ -207,55 +319,57 @@
     dec_out,
 ):
     n_lat, n_lon = lax.axis_size("lat"), lax.axis_size("lon")
-    packed = pl.pallas_call(
-        functools.partial(pack_kernel, n_lon),
-        out_shape=jax.ShapeDtypeStruct((n_lon, LEVELS, HALF, 128), F32),
-        in_specs=[VM],
-        out_specs=VM,
-        compiler_params=PARAMS,
-    )(level_tokens.transpose(0, 2, 3, 1))
-    got = lax.all_to_all(packed, "lon", split_axis=0, concat_axis=0, tiled=True)
     quad = jax.ShapeDtypeStruct((LATENT, QUAD, D), F32)
+    three = pltpu.VMEM((3, LATENT, QUAD, D), F32)
+    sems = pltpu.SemaphoreType.DMA
     q00, q01, q10, q11 = pl.pallas_call(
         agg_kernel,
         out_shape=[quad] * 4,
         in_specs=[VM] * 5,
         out_specs=[VM] * 4,
-        scratch_shapes=[pltpu.VMEM((LEVELS * 80, D), F32), pltpu.VMEM((LEVELS * 80, D), F32)],
-        compiler_params=PARAMS,
-    )(got, latent_queries, agg_key, agg_value, agg_out)
-
-    lon = [(j, (j - 1) % n_lon) for j in range(n_lon)]
-    lat = [(i, (i - 1) % n_lat) for i in range(n_lat)]
-    both = [
-        (i * n_lon + j, (i - 1) % n_lat * n_lon + (j - 1) % n_lon)
-        for i in range(n_lat)
-        for j in range(n_lon)
-    ]
-
-    def back(pairs):
-        return [(target, source) for source, target in pairs]
-
-    q00 = lax.ppermute(q00, ("lat", "lon"), both)
-    q01 = lax.ppermute(q01, "lat", lat)
-    q10 = lax.ppermute(q10, "lon", lon)
+        scratch_shapes=[
+            pltpu.VMEM((n_lon, LEVELS, HALF, 128), F32),
+            pltpu.VMEM((n_lon, LEVELS, HALF, 128), F32),
+            pltpu.VMEM((LEVELS, 80, D), F32),
+            pltpu.VMEM((LEVELS * 80, D), F32),
+            pltpu.VMEM((LEVELS, 80, LATENT * HEADS), F32),
+            pltpu.VMEM((D, D), BF16),
+            pltpu.VMEM((D, D), BF16),
+            three,
+            three,
+            sems((len(CHUNKS), n_lon)),
+            sems((len(CHUNKS), n_lon)),
+            sems((len(CHUNKS),)),
+            sems((3,)),
+            sems((3,)),
+        ],
+        compiler_params=pltpu.CompilerParams(
+            vmem_limit_bytes=LIMIT, collective_id=0, has_side_effects=True
+        ),
+    )(level_tokens.transpose(0, 2, 3, 1), latent_queries, agg_key, agg_value, agg_out)
     q11, q10, q01, q00 = pl.pallas_call(
         functools.partial(window_kernel, n_lat - 1),
         out_shape=[quad] * 4,
-        in_specs=[VM] * 10,
+        in_specs=[VM] * 8 + [pl.BlockSpec(memory_space=pl.ANY)] * 2,
         out_specs=[VM] * 4,
         scratch_shapes=[
             pltpu.VMEM((4 * QUAD * LATENT, 3 * D), F32),
             pltpu.VMEM((4 * QUAD * LATENT, D), F32),
+            pltpu.VMEM(mlp_in.shape, F32),
+            pltpu.VMEM(mlp_out.shape, F32),
+            three,
+            three,
+            sems((2,)),
+            sems((3,)),
+            sems((3,)),
         ],
-        compiler_params=PARAMS,
+        compiler_params=pltpu.CompilerParams(
+            vmem_limit_bytes=LIMIT, collective_id=1, has_side_effects=True
+        ),
     )(
         q11, q10, q01, q00, attn_gain.reshape(1, D), window_qkv, window_proj,
         mlp_gain.reshape(1, D), mlp_in, mlp_out,
     )
-    q00 = lax.ppermute(q00, ("lat", "lon"), back(both))
-    q01 = lax.ppermute(q01, "lat", back(lat))
-    q10 = lax.ppermute(q10, "lon", back(lon))
     return pl.pallas_call(
         decode_kernel,
         out_shape=jax.ShapeDtypeStruct((6, 12, LEVELS, D), F32),

time: 118 us -> 102 us (0.86)
  Pallas kernels: 57.3 us -> 102 us
  blocking collectives: 32.2 us -> 0 us
  waiting for transfers between devices: 21.2 us -> 0 us
  starting transfers between devices: 5.74 us -> 0 us
  local copies, waits for them, and re-layouts: 1.45 us -> 0 us
    pallas_call x1, Pallas kernels: 13.2 us -> 49.4 us  [on_device(): pl.pallas_call(agg_kernel, out_shape=[quad] * 4, in_specs=[VM] * 5, out_s...]
    all_to_all x1 -> x0, blocking collectives: 32.2 us -> none  [on_device(): got = lax.all_to_all(packed, 'lon', split_axis=0, concat_axis=0, tiled=True)]
    ppermute x6 -> x0, waiting for transfers between devices: 21.2 us -> none  [the longest x1 9.79 us: on_device(): q00 = lax.ppermute(q00, ('lat', 'lon'), back(both))]
    pallas_call x1, Pallas kernels: 27.7 us -> 39.9 us  [on_device(): pl.pallas_call(functools.partial(window_kernel, n_lat - 1), out_shape=[qu...]
    ppermute x6 -> x0, starting transfers between devices: 5.74 us -> none  [the longest x1 4.12 us: on_device(): q01 = lax.ppermute(q01, 'lat', lat)]
    pallas_call x1 -> x0, Pallas kernels: 3.78 us -> none  [on_device(): pl.pallas_call(functools.partial(pack_kernel, n_lon), out_shape=jax.Shape...]
    unnamed x12 -> x0, local copies, waits for them, and re-layouts: 1.45 us -> none
  transfers between devices with their start and end apart: 6 -> 0, of which waited for: 4 -> 0; matrix products, arithmetic and copies ran while one was open for 0% -> 0% of each run, Pallas kernels for 0% -> 0%
where the time goes in v1:
time: 102 us
  Pallas kernels  102 us (100%)
    pallas_call x1, Pallas kernels, on_device(): pl.pallas_call(agg_kernel, out_shape=[quad] * 4, in_specs=[VM] * 5, out_s...  49.4 us
    pallas_call x1, Pallas kernels, on_device(): pl.pallas_call(functools.partial(window_kernel, n_lat - 1), out_shape=[qu...  39.9 us
    pallas_call x1, Pallas kernels, on_device(): pl.pallas_call(decode_kernel, out_shape=jax.ShapeDtypeStruct((6, 12, LEVE...  12.7 us

profile of v1, /device:TPU:0, one launch (start us, length us, event | category | flops | bytes accessed | tf_op | source)
XLA Modules:
  0.0 102.0 jit_solution(17801491208268890221)
XLA Ops:
  0.0 49.4 %shard_map.145 = (f32[4,24,512]{2,1,0:T(8,128)}, f32[4,24,512]{2,1,0:T(8,128)}, f32[4,24,512]{2,1,0:T(8,128)}, f32[4,24,512]{2,1,0:T(8,128)}) custom-call(f32[6,13,64,96]{3,2,1,0:T(8,128)} %bitcast.3, f32[4,512]{1,0:T(4,128)} %queries.2, f32[512,512]{1,0:T(8,128)} %key.2, f32[512,512]{1,0:T(8,128)} %value.2, f32[512,512]{1,0:T(8,128)} %out_w.2), custom_call_target="tpu_custom_call" | custom-call | tf_op jit(solution)/shard_map/pallas_call | solution.py:325
  49.4 39.9 %shard_map.146 = (f32[4,24,512]{2,1,0:T(8,128)}, f32[4,24,512]{2,1,0:T(8,128)}, f32[4,24,512]{2,1,0:T(8,128)}, f32[4,24,512]{2,1,0:T(8,128)}) custom-call(f32[4,24,512]{2,1,0:T(8,128)} %get-tuple-element.13.q11, f32[4,24,512]{2,1,0:T(8,128)} %get-tuple-element.14.q10, f32[4,24,512]{2,1,0:T(8,128)} %get-tuple-element.15.q01, ...), custom_call_target="tpu_custom_call" | custom-call | tf_op jit(solution)/shard_map/pallas_call | solution.py:350
  89.3 12.7 %shard_map.147 = f32[6,12,13,512]{3,2,1,0:T(8,128)} custom-call(f32[4,24,512]{2,1,0:T(8,128)} %get-tuple-element.17.q00, f32[4,24,512]{2,1,0:T(8,128)} %get-tuple-element.18.q01, f32[4,24,512]{2,1,0:T(8,128)} %get-tuple-element.19.q10, f32[4,24,512]{2,1,0:T(8,128)} %get-tuple-element.20.q11, f32[13,512]{1,0:T(8,128)} %queries.3, f32[512,512]{1,0:T(8,128)} %key.3, ...), custom_call_target="tpu_custom_call" | custom-call | tf_op jit(solution)/shard_map/pallas_call | solution.py:373

commit v2 on v1

--- a/solution.py
+++ b/solution.py
@@ -32,9 +32,27 @@
 
 
 def dot3(a, b):
+    bh, bl = split(b)
     ah, al = split(a)
-    bh, bl = split(b)
-    return mm(ah, bh) + (mm(ah, bl) + mm(al, bh))
+    return mm(jnp.concatenate([ah, ah], 1), jnp.concatenate([bh, bl], 0)) + mm(al, bh)
+
+
+def dot3_stored(a, pair):
+    ah, al = split(a)
+    return mm(jnp.concatenate([ah, ah], 1), pair[...]) + mm(al, pair[: a.shape[1]])
+
+
+def store_pair(pair, ref):
+    step = 128
+
+    def body(i, carry):
+        at = pl.multiple_of(i * step, step)
+        hi, lo = split(ref[pl.ds(at, step), :])
+        pair[pl.ds(at, step), :] = hi
+        pair[pl.ds(pl.multiple_of(at + ref.shape[0], step), step), :] = lo
+        return carry
+
+    lax.fori_loop(0, ref.shape[0] // step, body, 0)
 
 
 def dot6(a, b):
@@ -106,10 +124,27 @@
 
 
 def agg_kernel(
-    tokens, queries, key, value, out_w, q00, q01, q10, q11,
-    packed, got, tok, val, score, vhi, vlo, sent, landed,
-    pack_send, pack_recv, own_sem, quad_send, quad_recv,
+    last, tokens, queries, key, attn_gain, mlp_gain, level_queries, dec_key,
+    hbm_value, hbm_out_w, hbm_qkv, hbm_proj, hbm_in, hbm_out,
+    o00, o01, o10, o11, dec_fold,
+    packed, got, tok, val, score, q11, sent, landed, joined, att, sent2, landed2,
+    value32, out_w32, qkv32, proj32, in32, out32, value, out_w, qkv, proj, mlp_in, mlp_out,
+    pack_send, pack_recv, own_sem, quad_send, quad_recv, quad_send2, quad_recv2, load_sem,
 ):
+    stored = (
+        (hbm_value, value32, value),
+        (hbm_out_w, out_w32, out_w),
+        (hbm_qkv, qkv32, qkv),
+        (hbm_proj, proj32, proj),
+        (hbm_in, in32, mlp_in),
+        (hbm_out, out32, mlp_out),
+    )
+    loads = [
+        pltpu.make_async_copy(source, stage, load_sem.at[i])
+        for i, (source, stage, _) in enumerate(stored)
+    ]
+    for load in loads:
+        load.start()
     count = lax.axis_size("lon")
     a, b = lax.axis_index("lat"), lax.axis_index("lon")
     partners = [(a, lax.rem(b + k, count)) for k in range(1, count)]
@@ -173,19 +208,22 @@
             remote(c, k).start()
         own(c).start()
     fold = folded(key[...], queries[...], LATENT)
-    vhi[...], vlo[...] = split(value[...])
+    dec_fold[...] = folded(dec_key[...], level_queries[...], LEVELS)
+    for load, (_, stage, pair) in zip(loads, stored):
+        load.wait()
+        store_pair(pair, stage)
     lane = lax.broadcasted_iota(jnp.int32, (HALF, 128), 1) // channels
 
     def unpack_level(level, carry):
         for t in range(4):
             for g in range(2):
-                joined = jnp.zeros((HALF, 128), F32)
+                block_all = jnp.zeros((HALF, 128), F32)
                 for i in range(ways):
                     block = got[ways * t + i, level]
                     if i != g:
                         block = pltpu.roll(block, (i - g) * channels % 128, 1)
-                    joined = jnp.where(lane == i, block, joined)
-                tok[level, g * HALF : g * HALF + HALF, 128 * t : 128 * t + 128] = joined
+                    block_all = jnp.where(lane == i, block, block_all)
+                tok[level, g * HALF : g * HALF + HALF, 128 * t : 128 * t + 128] = block_all
         return carry
 
     for c, (low, high) in enumerate(CHUNKS):
@@ -195,9 +233,7 @@
         lax.fori_loop(low, high, unpack_level, 0)
         x = tok[low:high].reshape((high - low) * 80, D)
         score[low:high] = dot6(x, fold).reshape(high - low, 80, LATENT * HEADS)
-        xh, xl = split(x)
-        v = mm(xh, vhi[...]) + (mm(xh, vlo[...]) + mm(xl, vhi[...]))
-        val[low * 80 : high * 80] = v
+        val[low * 80 : high * 80] = dot3_stored(x, value)
     scores = score[...]
     expo = jnp.exp(scores - jnp.max(scores, axis=0, keepdims=True))
     weights = (expo / jnp.sum(expo, axis=0, keepdims=True)).reshape(LEVELS * 80, LATENT * HEADS)
@@ -207,7 +243,7 @@
         spread = widen(c, LATENT * HEADS)
         wide = (mm(wh, spread) + mm(wl, spread)) * val[...]
         mixed.append(jnp.sum(wide.reshape(LEVELS, 80, D), axis=0))
-    latent = dot3(jnp.concatenate(mixed, axis=0), out_w[...])
+    latent = dot3_stored(jnp.concatenate(mixed, axis=0), out_w)
     for c in range(LATENT):
         for i, ref in enumerate((sent.at[0], sent.at[1], sent.at[2], q11)):
             base = c * 80 + i // 2 * HALF + i % 2 * 18
@@ -217,27 +253,14 @@
     for c in range(len(CHUNKS)):
         for k in order:
             remote(c, k).wait_send()
-    for copy, i, ref in zip(copies, range(3), (q00, q01, q10)):
+    for copy in copies:
         copy.wait()
-        ref[...] = landed[i]
-
-
-def window_kernel(
-    last, q11, q10, q01, q00, attn_gain, qkv, proj, mlp_gain, hbm_in, hbm_out, o11, o10, o01, o00,
-    joined, att, mlp_in, mlp_out, sent, landed, load_sem, quad_send, quad_recv,
-):
-    loads = [
-        pltpu.make_async_copy(hbm_in, mlp_in, load_sem.at[0]),
-        pltpu.make_async_copy(hbm_out, mlp_out, load_sem.at[1]),
-    ]
-    for load in loads:
-        load.start()
-    greet(list(places(-1)) + list(places(1)))
+    q00, q01, q10 = landed.at[0], landed.at[1], landed.at[2]
     side = 4 * QUAD
     latent = jnp.concatenate(
         [ref[c] for c in range(LATENT) for ref in (q11, q10, q01, q00)], axis=0
     )
-    joined[...] = dot3(layer_norm(latent, attn_gain[...]), qkv[...])
+    joined[...] = dot3_stored(layer_norm(latent, attn_gain[...]), qkv)
     edge = lax.axis_index("lat") == last
     for c0, depth in ((0, 1), (1, 2), (3, 1)):
         n = side * depth
@@ -252,38 +275,39 @@
             v = joined[rows, 2 * D + 128 * t : 2 * D + 128 * t + 128]
             kh, kl = split(k)
             vh, vl = split(v)
+            khh = jnp.concatenate([kh, kh], 1)
+            vhl = jnp.concatenate([vh, vl], 1)
             total = jnp.zeros((n, 128), F32)
             for h in range(4):
                 mine = head_of((n, 128), 1) == h
                 qh, ql = split(jnp.where(mine, q, 0.0))
                 nt = (((1,), (1,)), ((), ()))
-                s = mm(qh, kh, nt) + (mm(qh, kl, nt) + mm(ql, kh, nt))
+                s = mm(jnp.concatenate([qh, ql], 1), khh, nt) + mm(qh, kl, nt)
                 s = jnp.where(ok, s, -1e30)
                 e = jnp.exp(s - jnp.max(s, -1, keepdims=True))
                 eh, el = split(e)
-                r = mm(eh, vh) + (mm(eh, vl) + mm(el, vh))
+                r = mm(eh, vhl)
+                r = r[:, :128] + (r[:, 128:] + mm(el, vh))
                 total = jnp.where(mine, r / jnp.sum(e, -1, keepdims=True), total)
             att[rows, 128 * t : 128 * t + 128] = total
-    mid = latent + dot3(att[...], proj[...])
-    for load in loads:
-        load.wait()
-    hidden = jax.nn.gelu(dot3(layer_norm(mid, mlp_gain[...]), mlp_in[...]))
-    done = mid + dot3(hidden, mlp_out[...])
+    mid = latent + dot3_stored(att[...], proj)
+    hidden = jax.nn.gelu(dot3_stored(layer_norm(mid, mlp_gain[...]), mlp_in))
+    done = mid + dot3_stored(hidden, mlp_out)
     for c in range(LATENT):
-        for i, ref in enumerate((o11, sent.at[2], sent.at[1], sent.at[0])):
+        for i, ref in enumerate((o11, sent2.at[2], sent2.at[1], sent2.at[0])):
             base = c * side + i * QUAD
             ref[c] = done[base : base + QUAD]
-    copies = hand_over(1, sent, landed, quad_send, quad_recv)
+    copies = hand_over(1, sent2, landed2, quad_send2, quad_recv2)
     for copy, i, ref in zip(copies, range(3), (o00, o01, o10)):
         copy.wait()
-        ref[...] = landed[i]
-
-
-def decode_kernel(q00, q01, q10, q11, queries, key, value, out_w, out, mixed):
+        ref[...] = landed2[i]
+
+
+def decode_kernel(q00, q01, q10, q11, fold, value, out_w, out, mixed):
     side = 4 * QUAD
     x = jnp.concatenate([ref[c] for c in range(LATENT) for ref in (q00, q01, q10, q11)], axis=0)
     width = LEVELS * HEADS
-    scores = dot6(x, folded(key[...], queries[...], LEVELS)).reshape(LATENT, side, width)
+    scores = dot6(x, fold[...]).reshape(LATENT, side, width)
     val = dot3(x, value[...])
     expo = jnp.exp(scores - jnp.max(scores, axis=0, keepdims=True))
     weights = (expo / jnp.sum(expo, axis=0, keepdims=True)).reshape(LATENT * side, width)
@@ -322,62 +346,51 @@
     quad = jax.ShapeDtypeStruct((LATENT, QUAD, D), F32)
     three = pltpu.VMEM((3, LATENT, QUAD, D), F32)
     sems = pltpu.SemaphoreType.DMA
-    q00, q01, q10, q11 = pl.pallas_call(
-        agg_kernel,
-        out_shape=[quad] * 4,
-        in_specs=[VM] * 5,
-        out_specs=[VM] * 4,
+    stored = (agg_value, agg_out, window_qkv, window_proj, mlp_in, mlp_out)
+    q00, q01, q10, q11, fold = pl.pallas_call(
+        functools.partial(agg_kernel, n_lat - 1),
+        out_shape=[quad] * 4 + [jax.ShapeDtypeStruct((D, LEVELS * HEADS), F32)],
+        in_specs=[VM] * 7 + [pl.BlockSpec(memory_space=pl.ANY)] * 6,
+        out_specs=[VM] * 5,
         scratch_shapes=[
             pltpu.VMEM((n_lon, LEVELS, HALF, 128), F32),
             pltpu.VMEM((n_lon, LEVELS, HALF, 128), F32),
             pltpu.VMEM((LEVELS, 80, D), F32),
             pltpu.VMEM((LEVELS * 80, D), F32),
             pltpu.VMEM((LEVELS, 80, LATENT * HEADS), F32),
-            pltpu.VMEM((D, D), BF16),
-            pltpu.VMEM((D, D), BF16),
+            pltpu.VMEM((LATENT, QUAD, D), F32),
             three,
             three,
+            pltpu.VMEM((4 * QUAD * LATENT, 3 * D), F32),
+            pltpu.VMEM((4 * QUAD * LATENT, D), F32),
+            three,
+            three,
+            *[pltpu.VMEM(w.shape, F32) for w in stored],
+            *[pltpu.VMEM((2 * w.shape[0], w.shape[1]), BF16) for w in stored],
             sems((len(CHUNKS), n_lon)),
             sems((len(CHUNKS), n_lon)),
             sems((len(CHUNKS),)),
             sems((3,)),
             sems((3,)),
+            sems((3,)),
+            sems((3,)),
+            sems((6,)),
         ],
         compiler_params=pltpu.CompilerParams(
             vmem_limit_bytes=LIMIT, collective_id=0, has_side_effects=True
         ),
-    )(level_tokens.transpose(0, 2, 3, 1), latent_queries, agg_key, agg_value, agg_out)
-    q11, q10, q01, q00 = pl.pallas_call(
-        functools.partial(window_kernel, n_lat - 1),
-        out_shape=[quad] * 4,
-        in_specs=[VM] * 8 + [pl.BlockSpec(memory_space=pl.ANY)] * 2,
-        out_specs=[VM] * 4,
-        scratch_shapes=[
-            pltpu.VMEM((4 * QUAD * LATENT, 3 * D), F32),
-            pltpu.VMEM((4 * QUAD * LATENT, D), F32),
-            pltpu.VMEM(mlp_in.shape, F32),
-            pltpu.VMEM(mlp_out.shape, F32),
-            three,
-            three,
-            sems((2,)),
-            sems((3,)),
-            sems((3,)),
-        ],
-        compiler_params=pltpu.CompilerParams(
-            vmem_limit_bytes=LIMIT, collective_id=1, has_side_effects=True
-        ),
     )(
-        q11, q10, q01, q00, attn_gain.reshape(1, D), window_qkv, window_proj,
-        mlp_gain.reshape(1, D), mlp_in, mlp_out,
+        level_tokens.transpose(0, 2, 3, 1), latent_queries, agg_key, attn_gain.reshape(1, D),
+        mlp_gain.reshape(1, D), level_queries, dec_key, *stored,
     )
     return pl.pallas_call(
         decode_kernel,
         out_shape=jax.ShapeDtypeStruct((6, 12, LEVELS, D), F32),
-        in_specs=[VM] * 8,
+        in_specs=[VM] * 7,
         out_specs=VM,
         scratch_shapes=[pltpu.VMEM((LEVELS * 4 * QUAD, D), F32)],
         compiler_params=PARAMS,
-    )(q00, q01, q10, q11, level_queries, dec_key, dec_value, dec_out)
+    )(q00, q01, q10, q11, fold, dec_value, dec_out)
 
 
 def solution(mesh):

time: 102 us -> 90.3 us (0.89)
  Pallas kernels: 102 us -> 90.2 us
    pallas_call x2 -> x1, Pallas kernels: 89.3 us -> 80 us  [on_device(): pl.pallas_call(functools.partial(agg_kernel, n_lat - 1), out_shape=[quad]...]
    pallas_call x1, Pallas kernels: 12.7 us -> 10.2 us  [on_device(): pl.pallas_call(decode_kernel, out_shape=jax.ShapeDtypeStruct((6, 12, LEVE...]
where the time goes in v2:
time: 90.3 us; the launch traced here: 90.2 us
  Pallas kernels  90.2 us (100%)
    pallas_call x1, Pallas kernels, on_device(): pl.pallas_call(functools.partial(agg_kernel, n_lat - 1), out_shape=[quad]...  80 us
    pallas_call x1, Pallas kernels, on_device(): pl.pallas_call(decode_kernel, out_shape=jax.ShapeDtypeStruct((6, 12, LEVE...  10.2 us

profile of v2, /device:TPU:0, one launch (start us, length us, event | category | flops | bytes accessed | tf_op | source)
XLA Modules:
  0.0 90.2 jit_solution(16959555671104250344)
XLA Ops:
  0.0 80.0 %shard_map.145 = (f32[4,24,512]{2,1,0:T(8,128)}, f32[4,24,512]{2,1,0:T(8,128)}, f32[4,24,512]{2,1,0:T(8,128)}, f32[4,24,512]{2,1,0:T(8,128)}, f32[512,208]{1,0:T(8,128)}) custom-call(f32[6,13,64,96]{3,2,1,0:T(8,128)} %bitcast.3, f32[4,512]{1,0:T(4,128)} %queries.1, f32[512,512]{1,0:T(8,128)} %key.1, f32[1,512]{1,0:T(1,128)} %bitcast.4, f32[1,512]{1,0:T(1,128)} %bitcast.5, ...), custom_call_target="tpu_custom_call" | custom-call | tf_op jit(solution)/shard_map/pallas_call | solution.py:350
  80.0 10.2 %shard_map.146 = f32[6,12,13,512]{3,2,1,0:T(8,128)} custom-call(f32[4,24,512]{2,1,0:T(8,128)} %get-tuple-element.10.q00, f32[4,24,512]{2,1,0:T(8,128)} %get-tuple-element.11.q01, f32[4,24,512]{2,1,0:T(8,128)} %get-tuple-element.12.q10, f32[4,24,512]{2,1,0:T(8,128)} %get-tuple-element.13.q11, f32[512,208]{1,0:T(8,128)} %get-tuple-element.14.fold, ...), custom_call_target="tpu_custom_call" | custom-call | tf_op jit(solution)/shard_map/pallas_call | solution.py:386

commit v3 on v2

--- a/solution.py
+++ b/solution.py
@@ -291,15 +291,29 @@
                 total = jnp.where(mine, r / jnp.sum(e, -1, keepdims=True), total)
             att[rows, 128 * t : 128 * t + 128] = total
     mid = latent + dot3_stored(att[...], proj)
-    hidden = jax.nn.gelu(dot3_stored(layer_norm(mid, mlp_gain[...]), mlp_in))
-    done = mid + dot3_stored(hidden, mlp_out)
-    for c in range(LATENT):
-        for i, ref in enumerate((o11, sent2.at[2], sent2.at[1], sent2.at[0])):
-            base = c * side + i * QUAD
-            ref[c] = done[base : base + QUAD]
-    copies = hand_over(1, sent2, landed2, quad_send2, quad_recv2)
-    for copy, i, ref in zip(copies, range(3), (o00, o01, o10)):
-        copy.wait()
+    flights = []
+    for p in range(2):
+        part = mid[2 * p * side : 2 * (p + 1) * side]
+        hidden = jax.nn.gelu(dot3_stored(layer_norm(part, mlp_gain[...]), mlp_in))
+        done = part + dot3_stored(hidden, mlp_out)
+        for c in range(2):
+            for i, ref in enumerate((o11, sent2.at[2], sent2.at[1], sent2.at[0])):
+                base = c * side + i * QUAD
+                ref[2 * p + c] = done[base : base + QUAD]
+        for i, device in enumerate(places(1)):
+            flight = pltpu.make_async_remote_copy(
+                src_ref=sent2.at[i, 2 * p : 2 * p + 2],
+                dst_ref=landed2.at[i, 2 * p : 2 * p + 2],
+                send_sem=quad_send2.at[p, i],
+                recv_sem=quad_recv2.at[p, i],
+                device_id=device,
+                device_id_type=MESH,
+            )
+            flight.start()
+            flights.append(flight)
+    for flight in flights:
+        flight.wait()
+    for i, ref in enumerate((o00, o01, o10)):
         ref[...] = landed2[i]
 
 
@@ -372,8 +386,8 @@
             sems((len(CHUNKS),)),
             sems((3,)),
             sems((3,)),
-            sems((3,)),
-            sems((3,)),
+            sems((2, 3)),
+            sems((2, 3)),
             sems((6,)),
         ],
         compiler_params=pltpu.CompilerParams(

time: 90.3 us -> 87.7 us (0.971)
  Pallas kernels: 90.2 us -> 87.6 us
    pallas_call x1, Pallas kernels: 80 us -> 77.4 us  [on_device(): pl.pallas_call(functools.partial(agg_kernel, n_lat - 1), out_shape=[quad]...]
where the time goes in v3:
time: 87.7 us; the launch traced here: 87.6 us
  Pallas kernels  87.6 us (100%)
    pallas_call x1, Pallas kernels, on_device(): pl.pallas_call(functools.partial(agg_kernel, n_lat - 1), out_shape=[quad]...  77.4 us
    pallas_call x1, Pallas kernels, on_device(): pl.pallas_call(decode_kernel, out_shape=jax.ShapeDtypeStruct((6, 12, LEVE...  10.2 us

profile of v3, /device:TPU:0, one launch (start us, length us, event | category | flops | bytes accessed | tf_op | source)
XLA Modules:
  0.0 87.6 jit_solution(9666157786575058729)
XLA Ops:
  0.0 77.4 %shard_map.145 = (f32[4,24,512]{2,1,0:T(8,128)}, f32[4,24,512]{2,1,0:T(8,128)}, f32[4,24,512]{2,1,0:T(8,128)}, f32[4,24,512]{2,1,0:T(8,128)}, f32[512,208]{1,0:T(8,128)}) custom-call(f32[6,13,64,96]{3,2,1,0:T(8,128)} %bitcast.3, f32[4,512]{1,0:T(4,128)} %queries.1, f32[512,512]{1,0:T(8,128)} %key.1, f32[1,512]{1,0:T(1,128)} %bitcast.4, f32[1,512]{1,0:T(1,128)} %bitcast.5, ...), custom_call_target="tpu_custom_call" | custom-call | tf_op jit(solution)/shard_map/pallas_call | solution.py:364
  77.4 10.2 %shard_map.146 = f32[6,12,13,512]{3,2,1,0:T(8,128)} custom-call(f32[4,24,512]{2,1,0:T(8,128)} %get-tuple-element.10.q00, f32[4,24,512]{2,1,0:T(8,128)} %get-tuple-element.11.q01, f32[4,24,512]{2,1,0:T(8,128)} %get-tuple-element.12.q10, f32[4,24,512]{2,1,0:T(8,128)} %get-tuple-element.13.q11, f32[512,208]{1,0:T(8,128)} %get-tuple-element.14.fold, ...), custom_call_target="tpu_custom_call" | custom-call | tf_op jit(solution)/shard_map/pallas_call | solution.py:400
